TPU v7x, 32 devices: a whole 2x2x4 slice. The times are simulated.
32 devices in a mesh: req: 16 (over z, y, x), tp: 2 (over core).
Axes of the slice: x: 2, y: 2, z: 4, core: 2. Of those that a mesh axis runs over, the one named last changes fastest.
Arguments:
- residual: bfloat16 [512, 2048], P('req'), may hold values from -6 to 6
- fresh_qkv: bfloat16 [512, 3, 2048], P('req', None, 'tp'), may hold values from -32 to 32
- kv_cache: bfloat16 [512, 24, 2, 2048], P('req', None, None, 'tp'), may hold values from -32 to 32
- cache_len: int32 [512], P('req'), may hold values from 2 to 24, as said below
- out_proj: bfloat16 [2048, 2048], P('tp'), may hold values from -0.125 to 0.125
- norm_gain: float32 [2048], replicated, may hold values from 0.1 to 1.9
- router_weight: float32 [2048, 16], replicated, may hold values from -7.9549513 to 7.9549513
- expert_ids: int32 [512, 8], P('req'), may hold values from 0 to 15, all different within a row; in each aligned block of 32 rows (0 to 31, 32 to 63, ...) at most 32 rows name the same one
- gate_up: bfloat16 [16, 2048, 2, 1024], P('req', None, None, 'tp'), may hold values from -0.125 to 0.125
- down_proj: bfloat16 [16, 1024, 2048], P('req', 'tp'), may hold values from -0.1875 to 0.1875
Outputs:
- layer_out: bfloat16 [512, 2048], P('req', 'tp')
Inputs may be any that keep to these rules, and one draw needn't show every extreme that they name: `expert_ids`: each row names 8 different experts; among the 32 rows of one device no expert is named by more than 32 rows, and some device reaches 32. `cache_len`: some request uses all 24 positions.
All inputs are finite; a program needn't handle non-finite values.
Results may differ from a plain program's by a relative error of at most 0.018.
Values may be sent and summed in bfloat16 or wider, within the bound.
A program may use at most 128 MiB of HBM per device.

v0:
```python
import jax
import jax.numpy as jnp
from jax import lax
from jax.sharding import PartitionSpec as P

HD = 128


def rms_normed(hidden_in, gain):
    values = hidden_in.astype(jnp.float32)
    scale_inv = lax.rsqrt(jnp.mean(values * values, axis=-1, keepdims=True) + 1e-05)
    return (values * scale_inv * gain).astype(jnp.bfloat16)


def attend(fresh_qkv, kv_cache, cache_len):
    requests, ctx_len = (kv_cache.shape[0], kv_cache.shape[1])
    local_heads = fresh_qkv.shape[2] // HD
    queries = fresh_qkv[:, 0].reshape(requests, local_heads, HD)
    new_keys = fresh_qkv[:, 1].reshape(requests, local_heads, HD)
    new_values = fresh_qkv[:, 2].reshape(requests, local_heads, HD)
    cache_keys = kv_cache[:, :, 0].reshape(requests, ctx_len, local_heads, HD)
    cache_values = kv_cache[:, :, 1].reshape(requests, ctx_len, local_heads, HD)
    factor = HD ** (-0.5)
    scores = (
        jnp.einsum("nhd,nchd->nhc", queries, cache_keys, preferred_element_type=jnp.float32)
        * factor
    )
    own_score = (
        jnp.einsum("nhd,nhd->nh", queries, new_keys, preferred_element_type=jnp.float32) * factor
    )
    valid = (jnp.arange(ctx_len, dtype=jnp.int32)[None, :] < cache_len[:, None])[:, None, :]
    masked = jnp.where(valid, scores, -jnp.inf)
    top_score = jnp.maximum(jnp.max(masked, axis=-1), own_score)
    expos = jnp.where(valid, jnp.exp(masked - top_score[..., None]), 0.0)
    own_expo = jnp.exp(own_score - top_score)
    total = jnp.sum(expos, axis=-1) + own_expo
    weights = (expos / total[..., None]).astype(jnp.bfloat16)
    own_weight = (own_expo / total).astype(jnp.bfloat16)
    mixed = jnp.einsum("nhc,nchd->nhd", weights, cache_values, preferred_element_type=jnp.float32)
    mixed = mixed + own_weight.astype(jnp.float32)[..., None] * new_values.astype(jnp.float32)
    return mixed.astype(jnp.bfloat16).reshape(requests, local_heads * HD)


def local(
    residual,
    fresh_qkv,
    kv_cache,
    cache_len,
    out_proj,
    norm_gain,
    router_weight,
    expert_ids,
    gate_up,
    down_proj,
):
    tp_place = lax.axis_index("tp")
    me = lax.axis_index("req")
    experts = lax.axis_size("req")
    attended = attend(fresh_qkv, kv_cache, cache_len)
    partial_value = jnp.dot(attended, out_proj, preferred_element_type=jnp.float32)
    summed = lax.psum(partial_value, "tp")
    hidden = (residual.astype(jnp.float32) + summed).astype(jnp.bfloat16)
    normed = rms_normed(hidden, norm_gain)
    rows = lax.all_gather(normed, "req", axis=0, tiled=True)
    logits = jnp.dot(normed.astype(jnp.float32), router_weight, precision=lax.Precision.HIGHEST)
    named = jnp.any(
        expert_ids[:, :, None] == jnp.arange(experts, dtype=jnp.int32)[None, None, :], axis=1
    )
    gates = jax.nn.softmax(jnp.where(named, logits, -jnp.inf), axis=-1)
    gates_all = lax.all_gather(gates, "req", axis=0, tiled=True)
    mine = jnp.arange(experts, dtype=jnp.int32)[None, :] == me
    weight = jnp.sum(jnp.where(mine, gates_all, 0.0), axis=1, keepdims=True)
    gate_part = jnp.dot(rows, gate_up[0, :, 0], preferred_element_type=jnp.float32)
    up_part = jnp.dot(rows, gate_up[0, :, 1], preferred_element_type=jnp.float32)
    inner = (jax.nn.silu(gate_part) * up_part).astype(jnp.bfloat16)
    result = jnp.dot(inner, down_proj[0], preferred_element_type=jnp.float32)
    own = lax.psum_scatter(result * weight, "tp", scatter_dimension=1, tiled=True)
    moe_share = lax.psum_scatter(own, "req", scatter_dimension=0, tiled=True)
    width_here = moe_share.shape[1]
    own_cols = lax.dynamic_slice_in_dim(hidden, tp_place * width_here, width_here, 1)
    return (own_cols.astype(jnp.float32) + moe_share).astype(jnp.bfloat16)


def solution(mesh):
    in_specs = (
        P("req", None),
        P("req", None, "tp"),
        P("req", None, None, "tp"),
        P("req"),
        P("tp", None),
        P(),
        P(),
        P("req", None),
        P("req", None, None, "tp"),
        P("req", "tp", None),
    )
    out_specs = P("req", "tp")
    return jax.shard_map(local, mesh=mesh, in_specs=in_specs, out_specs=out_specs, check_vma=False)
```

profile of v0, /device:TPU:0, one launch (start us, length us, event | category | flops | bytes accessed | tf_op | source)
XLA Modules:
  0.0 234.0 jit_solution(13227113264910571109)
XLA Ops:
  6.5 0.0 copy-start
  6.5 0.0 all-reduce.2.cloned.1.call-start
  6.5 0.8 iota_compare_fusion.1
  7.4 0.9 convert_bitcast_fusion
  8.4 0.1 fusion.20
  8.5 0.1 copy.30
  8.5 0.1 reshape.54
  8.6 17.1 %slice_reduce_fusion = (bf16[32,24,1024]{2,1,0:T(8,128)(2,1)}, bf16[32,24,1024]{2,1,0:T(8,128)(2,1)S(1)}) fusion(bf16[32,24,2,1024]{3,2,1,0:T(2,128)(2,1)} %param.12), kind=kLoop, calls=%fused_computation.1 | loop fusion | bytes 6291456 | tf_op jit(solution)/shard_map/slice | solution.py:22
  25.7 0.9 fusion.6
  26.7 0.1 copy.26
  26.9 0.1 copy.20
  27.0 0.2 copy.31
  27.2 2.0 fusion.3
  29.2 0.1 fusion.19
  29.3 0.0 copy-start.2
  29.3 0.0 copy-start.4
  29.3 0.0 copy-start.5
  29.3 3.8 %fusion.24 = f32[32,2048]{1,0:T(8,128)} fusion(bf16[1024,2048]{1,0:T(8,128)(2,1)} %param.14, bf16[4,8,8,128]{3,2,1,0:T(8,128)(2,1)S(1)} %bitcast.84), kind=kOutput, calls=%fused_computation.40 | convolution fusion | flops 134217728 | bytes 4521984 | tf_op jit(solution)/shard_map/dot_general | solution.py:60
  33.1 0.0 all-reduce.2.cloned.1.call-update
  33.1 0.0 all-gather.3.cloned.1.call-start
  33.2 21.1 %all-reduce.2.cloned.1.call-done = f32[32,2048]{1,0:T(8,128)} async-done(((f32[32,2048]{1,0:T(8,128)}), f32[32,2048]{1,0:T(8,128)}) %all-reduce.2.cloned.1.call-update) | async-done | bytes 262160 | tf_op jit(solution)/shard_map/psum | solution.py:61
  54.3 0.0 copy-done.2
  54.3 1.1 fusion.15
  55.4 0.0 copy-done.4
  55.4 0.7 fusion.17
  56.1 0.0 all-gather.3.cloned.1.call-update
  56.1 0.0 reduce-scatter.3.cloned.1.call-start
  56.2 0.0 copy-done.5
  56.2 0.0 copy-start.1
  56.3 0.0 copy-start.3
  56.3 10.4 %fusion.33 = (bf16[1,2048,1,512]{3,2,1,0:T(2,128)(2,1)}, bf16[1,2048,1,512]{3,2,1,0:T(2,128)(2,1)}) fusion(bf16[1,2048,2,512]{3,2,1,0:T(2,128)(2,1)} %param.18), kind=kLoop, calls=%fused_computation.61 | loop fusion | bytes 8388608 | tf_op jit(solution)/shard_map/slice | solution.py:73
  66.7 0.0 copy-done.1
  66.7 0.0 copy-done.3
  66.7 0.2 fusion.34
  67.0 41.8 %all-gather = f32[16,32,16]{1,2,0:T(8,128)S(1)} all-gather(f32[1,32,16]{1,2,0:T(8,128)S(1)} %divide_bitcast_fusion), channel_id=1, replica_groups=mesh['req'=16,'tp'=2] {'req'}, dimensions={0}, use_global_device_ids=true | all-gather | bytes 34816 | tf_op jit(solution)/shard_map/all_gather | solution.py:70
  108.9 0.1 reshape.46
  109.0 0.1 select_reduce_fusion
  109.1 10.6 %all-gather.3.cloned.1.call-done = bf16[512,2048]{1,0:T(8,128)(2,1)} async-done(((bf16[32,2048]{1,0:T(8,128)(2,1)}), bf16[512,2048]{1,0:T(8,128)(2,1)}) %all-gather.3.cloned.1.call-update) | async-done | bytes 2097168 | tf_op jit(solution)/shard_map/all_gather | solution.py:64
  119.6 4.1 %fusion.1 = f32[512,512]{1,0:T(8,128)S(1)} fusion(bf16[512,2048]{1,0:T(8,128)(2,1)} %all-gather.3.cloned.1.call-done, bf16[1,2048,1,512]{3,2,1,0:T(2,128)(2,1)} %get-tuple-element.9), kind=kOutput, calls=%fused_computation.6 | convolution fusion | flops 1073741824 | bytes 5242880 | tf_op jit(solution)/shard_map/dot_general | solution.py:73
  123.7 0.0 copy-done
  123.7 7.3 %convolution_multiply_fusion = f32[512,2048]{1,0:T(8,128)} fusion(bf16[1,512,2048]{2,1,0:T(8,128)(2,1)S(1)} %copy-done, f32[512]{0:T(512)S(1)} %select_reduce_fusion, bf16[512,2048]{1,0:T(8,128)(2,1)} %all-gather.3.cloned.1.call-done, bf16[1,2048,1,512]{3,2,1,0:T(2,128)(2,1)} %get-tuple-element.10, f32[512,512]{1,0:T(8,128)S(1)} %fusion.1), kind=kOutput, calls=%fused_computation | convolution fusion | flops 2150105088 | bytes 11536384 | tf_op jit(solution)/shard_map/dot_general | solution.py:76
  131.0 0.0 reduce-scatter.3.cloned.1.call-update
  131.0 0.0 reduce-scatter.5.cloned.1.call-start
  131.1 10.8 %reduce-scatter.3.cloned.1.call-done = f32[512,1024]{1,0:T(8,128)} async-done(((f32[512,2048]{1,0:T(8,128)}), f32[512,1024]{1,0:T(8,128)}) %reduce-scatter.3.cloned.1.call-update) | async-done | bytes 2097168 | tf_op jit(solution)/shard_map/reduce_scatter | solution.py:77
  141.8 0.0 reduce-scatter.5.cloned.1.call-update
  141.9 84.1 %reduce-scatter.5.cloned.1.call-done = f32[32,1024]{1,0:T(8,128)} async-done(((f32[512,1024]{1,0:T(8,128)}), f32[32,1024]{1,0:T(8,128)}) %reduce-scatter.5.cloned.1.call-update) | async-done | bytes 131088 | tf_op jit(solution)/shard_map/reduce_scatter | solution.py:78
  226.0 1.5 add_convert_fusion.1
  (14 shorter events, 0.3 us)
Async XLA Ops:
  6.5 117.2 %copy-start = (bf16[1,512,2048]{2,1,0:T(8,128)(2,1)S(1)}, bf16[1,512,2048]{2,1,0:T(8,128)(2,1)}, u32[]{:S(2)}) copy-start(bf16[1,512,2048]{2,1,0:T(8,128)(2,1)} %param.19) | copy-start | bytes 6291460
  6.5 47.7 %all-reduce.2.cloned.1.call-start = ((), (), s32[]{:S(2)}) async-start(), calls=%async_computation.2 | async-start | bytes 524288 | tf_op jit(solution)/shard_map/psum | solution.py:61
  29.3 25.0 %copy-start.2 = (bf16[32,2048]{1,0:T(8,128)(2,1)S(1)}, bf16[32,2048]{1,0:T(8,128)(2,1)}, u32[]{:S(2)}) copy-start(bf16[32,2048]{1,0:T(8,128)(2,1)} %param.10) | copy-start | bytes 393220
  29.3 26.1 %copy-start.4 = (f32[2048]{0:T(1024)S(1)}, f32[2048]{0:T(1024)}, u32[]{:S(2)}) copy-start(f32[2048]{0:T(1024)} %param.15) | copy-start | bytes 24580
  29.3 26.9 %copy-start.5 = (s32[32,8]{0,1:T(8,128)S(1)}, s32[32,8]{0,1:T(8,128)}, u32[]{:S(2)}) copy-start(s32[32,8]{0,1:T(8,128)} %param.17) | copy-start | bytes 3076
  33.1 86.5 %all-gather.3.cloned.1.call-start = ((), (), s32[]{:S(2)}) async-start(), calls=%async_computation.3 | async-start | bytes 2228224 | tf_op jit(solution)/shard_map/all_gather | solution.py:64
  56.1 85.7 %reduce-scatter.3.cloned.1.call-start = ((), (), s32[]{:S(2)}) async-start(), calls=%async_computation.4 | async-start | bytes 6291456 | tf_op jit(solution)/shard_map/reduce_scatter | solution.py:77
  56.2 10.5 %copy-start.1 = (bf16[32,2048]{1,0:T(8,128)(2,1)S(1)}, bf16[32,2048]{1,0:T(8,128)(2,1)}, u32[]{:S(2)}) copy-start(bf16[32,2048]{1,0:T(8,128)(2,1)} %fusion.17) | copy-start | bytes 393220
  56.3 10.5 %copy-start.3 = (f32[2048,16]{0,1:T(8,128)S(1)}, f32[2048,16]{0,1:T(8,128)}, u32[]{:S(2)}) copy-start(f32[2048,16]{0,1:T(8,128)} %param.16) | copy-start | bytes 393220
  131.0 95.0 %reduce-scatter.5.cloned.1.call-start = ((), (), s32[]{:S(2)}) async-start(), calls=%async_computation.5 | async-start | bytes 2228224 | tf_op jit(solution)/shard_map/reduce_scatter | solution.py:78
Sparse Core Ops, SparseCore 0:
  33.3 20.9 all-reduce.1
  57.4 62.1 all-gather.2
  131.1 10.6 reduce-scatter.2
  144.0 81.9 reduce-scatter.4
where the time goes:
time: 234 us
  waiting for transfers between devices  127 us (54%)
  blocking collectives  41.8 us (18%)
  local copies, waits for them, and re-layouts  28.3 us (12%)
  matrix products  18.2 us (8%)
  between operations  13.3 us (6%)
  other arithmetic  5.64 us (2%)
    reduce_scatter x1, waiting for transfers between devices, local(): moe_share = lax.psum_scatter(own, 'req', scatter_dimension=0, tiled=True)  84.1 us
    all_gather x1, blocking collectives, local(): gates_all = lax.all_gather(gates, 'req', axis=0, tiled=True)  41.8 us
    psum x1, waiting for transfers between devices, local(): summed = lax.psum(partial_value, 'tp')  21.1 us
    slice x1, local copies, waits for them, and re-layouts, attend(): cache_values = kv_cache[:, :, 1].reshape(requests, ctx_len, local_heads, HD)  17.1 us
    reduce_scatter x1, waiting for transfers between devices, local(): lax.psum_scatter(result * weight, 'tp', scatter_dimension=1, tiled=True)  10.8 us
    all_gather x1, waiting for transfers between devices, local(): rows = lax.all_gather(normed, 'req', axis=0, tiled=True)  10.6 us
    slice x1, local copies, waits for them, and re-layouts, local(): gate_up[0, :, 0]  10.4 us
    dot_general x1, matrix products, local(): result = jnp.dot(inner, down_proj[0], preferred_element_type=jnp.float32)  7.25 us
  transfers between devices with their start and end apart: 4, of which 4 were waited for; matrix products, arithmetic and copies ran while one was open for 5% of the time, Pallas kernels for 0%

commit v1 on v0

--- a/solution.py
+++ b/solution.py
@@ -61,13 +61,16 @@
     summed = lax.psum(partial_value, "tp")
     hidden = (residual.astype(jnp.float32) + summed).astype(jnp.bfloat16)
     normed = rms_normed(hidden, norm_gain)
-    rows = lax.all_gather(normed, "req", axis=0, tiled=True)
     logits = jnp.dot(normed.astype(jnp.float32), router_weight, precision=lax.Precision.HIGHEST)
     named = jnp.any(
         expert_ids[:, :, None] == jnp.arange(experts, dtype=jnp.int32)[None, None, :], axis=1
     )
     gates = jax.nn.softmax(jnp.where(named, logits, -jnp.inf), axis=-1)
-    gates_all = lax.all_gather(gates, "req", axis=0, tiled=True)
+    rows, gates_all = jnp.split(
+        lax.all_gather(jnp.concatenate([normed, gates], axis=1), "req", axis=0, tiled=True),
+        [normed.shape[1]],
+        axis=1,
+    )
     mine = jnp.arange(experts, dtype=jnp.int32)[None, :] == me
     weight = jnp.sum(jnp.where(mine, gates_all, 0.0), axis=1, keepdims=True)
     gate_part = jnp.dot(rows, gate_up[0, :, 0], preferred_element_type=jnp.float32)

time: 234 us -> 254 us (1.085)
  waiting for transfers between devices: 127 us -> 185 us
  blocking collectives: 41.8 us -> 0 us
    all_gather x1, waiting for transfers between devices: 10.6 us -> 69.3 us  [local(): lax.all_gather(jnp.concatenate([normed, gates], axis=1), 'req', axis=0, t...]
    all_gather x1 -> x0, blocking collectives: 41.8 us -> none  [local(): gates_all = lax.all_gather(gates, 'req', axis=0, tiled=True)]
  transfers between devices with their start and end apart: 4 -> 4, of which waited for: 4 -> 4; matrix products, arithmetic and copies ran while one was open for 5% -> 4% of each run, Pallas kernels for 0% -> 0%
where the time goes in v1:
time: 254 us; the launch traced here: 253 us
  waiting for transfers between devices  185 us (73%)
  local copies, waits for them, and re-layouts  28.2 us (11%)
  matrix products  19.7 us (8%)
  between operations  13.3 us (5%)
  other arithmetic  6.96 us (3%)
    reduce_scatter x1, waiting for transfers between devices, local(): moe_share = lax.psum_scatter(own, 'req', scatter_dimension=0, tiled=True)  84 us
    all_gather x1, waiting for transfers between devices, local(): lax.all_gather(jnp.concatenate([normed, gates], axis=1), 'req', axis=0, t...  69.3 us
    psum x1, waiting for transfers between devices, local(): summed = lax.psum(partial_value, 'tp')  20.9 us
    slice x1, local copies, waits for them, and re-layouts, attend(): cache_values = kv_cache[:, :, 1].reshape(requests, ctx_len, local_heads, HD)  17.1 us
    reduce_scatter x1, waiting for transfers between devices, local(): lax.psum_scatter(result * weight, 'tp', scatter_dimension=1, tiled=True)  10.8 us
    slice x1, local copies, waits for them, and re-layouts, local(): gate_up[0, :, 0]  10.5 us
    dot_general x1, matrix products, local(): result = jnp.dot(inner, down_proj[0], preferred_element_type=jnp.float32)  7.94 us
  transfers between devices with their start and end apart: 4, of which 4 were waited for; matrix products, arithmetic and copies ran while one was open for 4% of the time, Pallas kernels for 0%

profile of v1, /device:TPU:0, one launch (start us, length us, event | category | flops | bytes accessed | tf_op | source)
XLA Modules:
  0.0 253.4 jit_solution(5270578605767197818)
XLA Ops:
  6.5 0.0 copy-start
  6.5 0.0 all-reduce.2.cloned.1.call-start
  6.5 0.8 iota_compare_fusion.1
  7.4 0.9 convert_bitcast_fusion
  8.4 0.1 fusion.29
  8.5 0.1 copy.28
  8.5 0.1 reshape.52
  8.6 17.1 %slice_reduce_fusion = (bf16[32,24,1024]{2,1,0:T(8,128)(2,1)}, bf16[32,24,1024]{2,1,0:T(8,128)(2,1)S(1)}) fusion(bf16[32,24,2,1024]{3,2,1,0:T(2,128)(2,1)} %param.12), kind=kLoop, calls=%fused_computation.5 | loop fusion | bytes 6291456 | tf_op jit(solution)/shard_map/slice | solution.py:22
  25.7 0.9 fusion.8
  26.7 0.1 copy.24
  26.9 0.1 copy.17
  27.0 0.2 copy.29
  27.2 0.0 copy-start.4
  27.2 0.0 copy-start.1
  27.2 2.0 fusion.5
  29.2 0.0 copy-start.3
  29.2 0.0 copy-start.2
  29.3 0.1 fusion.28
  29.4 3.7 %fusion.33 = f32[32,2048]{1,0:T(8,128)} fusion(bf16[1024,2048]{1,0:T(8,128)(2,1)} %param.14, bf16[4,8,8,128]{3,2,1,0:T(8,128)(2,1)S(1)} %bitcast.77), kind=kOutput, calls=%fused_computation.45 | convolution fusion | flops 134217728 | bytes 4521984 | tf_op jit(solution)/shard_map/dot_general | solution.py:60
  33.1 0.0 all-reduce.2.cloned.1.call-update
  33.1 0.0 all-gather.2.cloned.1.call-start
  33.2 0.0 copy-done.4
  33.2 0.1 copy.18
  33.3 20.9 %all-reduce.2.cloned.1.call-done = f32[32,2048]{1,0:T(8,128)} async-done(((f32[32,2048]{1,0:T(8,128)}), f32[32,2048]{1,0:T(8,128)}) %all-reduce.2.cloned.1.call-update) | async-done | bytes 262160 | tf_op jit(solution)/shard_map/psum | solution.py:61
  54.2 0.0 copy-done.1
  54.2 1.1 fusion.23
  55.3 0.0 copy-done.3
  55.3 0.1 fusion.39
  55.4 0.0 copy-done.2
  55.5 0.4 fusion.46
  55.9 0.2 fusion.41
  56.1 0.1 fusion.40
  56.2 0.7 pad_maximum_fusion
  56.9 0.0 all-gather.2.cloned.1.call-update
  56.9 0.0 reduce-scatter.3.cloned.1.call-start
  57.0 10.5 %fusion.45 = (bf16[1,2048,1,512]{3,2,1,0:T(2,128)(2,1)}, bf16[1,2048,1,512]{3,2,1,0:T(2,128)(2,1)}) fusion(bf16[1,2048,2,512]{3,2,1,0:T(2,128)(2,1)} %param.18), kind=kLoop, calls=%fused_computation.66 | loop fusion | bytes 8388608 | tf_op jit(solution)/shard_map/slice | solution.py:76
  67.5 69.3 %all-gather.2.cloned.1.call-done = f32[512,2064]{1,0:T(8,128)} async-done(((f32[32,2064]{1,0:T(8,128)}), f32[512,2064]{1,0:T(8,128)}) %all-gather.2.cloned.1.call-update) | async-done | bytes 4227088 | tf_op jit(solution)/shard_map/all_gather | solution.py:70
  136.7 1.1 fusion.26
  137.8 4.7 %fusion.2 = f32[512,512]{1,0:T(8,128)S(1)} fusion(f32[512,2064]{1,0:T(8,128)} %all-gather.2.cloned.1.call-done, bf16[1,2048,1,512]{3,2,1,0:T(2,128)(2,1)} %get-tuple-element.9), kind=kOutput, calls=%fused_computation.2 | convolution fusion | flops 1073741824 | bytes 7340032 | tf_op jit(solution)/shard_map/dot_general | solution.py:76
  142.5 0.0 copy-done
  142.5 7.9 %convolution_multiply_fusion = f32[512,2048]{1,0:T(8,128)} fusion(bf16[1,512,2048]{2,1,0:T(8,128)(2,1)S(1)} %copy-done, f32[512]{0:T(512)S(1)} %fusion.26, bf16[1,2048,1,512]{3,2,1,0:T(2,128)(2,1)} %get-tuple-element.10, f32[512,2064]{1,0:T(8,128)} %all-gather.2.cloned.1.call-done, f32[512,512]{1,0:T(8,128)S(1)} %fusion.2), kind=kOutput, calls=%fused_computation.4 | convolution fusion | flops 2150105088 | bytes 13633536 | tf_op jit(solution)/shard_map/dot_general | solution.py:79
  150.5 0.0 reduce-scatter.3.cloned.1.call-update
  150.5 0.0 reduce-scatter.5.cloned.1.call-start
  150.6 10.8 %reduce-scatter.3.cloned.1.call-done = f32[512,1024]{1,0:T(8,128)} async-done(((f32[512,2048]{1,0:T(8,128)}), f32[512,1024]{1,0:T(8,128)}) %reduce-scatter.3.cloned.1.call-update) | async-done | bytes 2097168 | tf_op jit(solution)/shard_map/reduce_scatter | solution.py:80
  161.3 0.0 reduce-scatter.5.cloned.1.call-update
  161.4 84.0 %reduce-scatter.5.cloned.1.call-done = f32[32,1024]{1,0:T(8,128)} async-done(((f32[512,1024]{1,0:T(8,128)}), f32[32,1024]{1,0:T(8,128)}) %reduce-scatter.5.cloned.1.call-update) | async-done | bytes 131088 | tf_op jit(solution)/shard_map/reduce_scatter | solution.py:81
  245.3 1.5 add_convert_fusion.1
  (11 shorter events, 0.2 us)
Async XLA Ops:
  6.5 136.0 %copy-start = (bf16[1,512,2048]{2,1,0:T(8,128)(2,1)S(1)}, bf16[1,512,2048]{2,1,0:T(8,128)(2,1)}, u32[]{:S(2)}) copy-start(bf16[1,512,2048]{2,1,0:T(8,128)(2,1)} %param.19) | copy-start | bytes 6291460
  6.5 47.7 %all-reduce.2.cloned.1.call-start = ((), (), s32[]{:S(2)}) async-start(), calls=%async_computation.2 | async-start | bytes 524288 | tf_op jit(solution)/shard_map/psum | solution.py:61
  27.2 6.0 %copy-start.4 = (s32[32,8]{0,1:T(8,128)S(1)}, s32[32,8]{0,1:T(8,128)}, u32[]{:S(2)}) copy-start(s32[32,8]{0,1:T(8,128)} %param.17) | copy-start | bytes 3076
  27.2 27.0 %copy-start.1 = (bf16[32,2048]{1,0:T(8,128)(2,1)S(1)}, bf16[32,2048]{1,0:T(8,128)(2,1)}, u32[]{:S(2)}) copy-start(bf16[32,2048]{1,0:T(8,128)(2,1)} %param.10) | copy-start | bytes 393220
  29.2 26.1 %copy-start.3 = (f32[2048]{0:T(1024)S(1)}, f32[2048]{0:T(1024)}, u32[]{:S(2)}) copy-start(f32[2048]{0:T(1024)} %param.15) | copy-start | bytes 24580
  29.2 26.2 %copy-start.2 = (f32[2048,16]{0,1:T(8,128)S(1)}, f32[2048,16]{0,1:T(8,128)}, u32[]{:S(2)}) copy-start(f32[2048,16]{0,1:T(8,128)} %param.16) | copy-start | bytes 393220
  33.1 103.6 %all-gather.2.cloned.1.call-start = ((), (), s32[]{:S(2)}) async-start(), calls=%async_computation.3 | async-start | bytes 4734976 | tf_op jit(solution)/shard_map/all_gather | solution.py:70
  56.9 104.4 %reduce-scatter.3.cloned.1.call-start = ((), (), s32[]{:S(2)}) async-start(), calls=%async_computation.4 | async-start | bytes 6291456 | tf_op jit(solution)/shard_map/reduce_scatter | solution.py:80
  150.5 94.8 %reduce-scatter.5.cloned.1.call-start = ((), (), s32[]{:S(2)}) async-start(), calls=%async_computation.5 | async-start | bytes 2228224 | tf_op jit(solution)/shard_map/reduce_scatter | solution.py:81
Sparse Core Ops, SparseCore 0:
  33.2 20.9 all-reduce.1
  57.3 79.3 all-gather.1
  150.6 10.6 reduce-scatter.2
  163.5 81.8 reduce-scatter.4
